TPU v7x, 32 devices: a whole 2x2x4 slice. The times are simulated.
32 devices in a mesh: branch: 2 (over x), head: 4 (over z), page: 4 (over y, core).
Axes of the slice: x: 2, y: 2, z: 4, core: 2. Of those that a mesh axis runs over, the one named last changes fastest.
Arguments:
- queries: bfloat16 [2048, 4096], P(('branch', 'page'), 'head'), may hold values from -6 to 6
- new_keys: bfloat16 [2048, 512], P(('branch', 'page'), 'head'), may hold values from -6 to 6
- new_values: bfloat16 [2048, 512], P(('branch', 'page'), 'head'), may hold values from -6 to 6
- cache_keys: bfloat16 [16, 64, 512], P(('branch', 'page'), None, 'head'), may hold values from -6 to 6
- cache_values: bfloat16 [16, 64, 512], P(('branch', 'page'), None, 'head'), may hold values from -6 to 6
- block_table: int32 [8, 4], P(('branch', 'page')), may hold values from 0 to 15, as said below
- ancestor_len: int32 [8], P(('branch', 'page')), may hold values from 64 to 256, as said below
- out_weight: bfloat16 [4096, 8192], P('head', 'page'), may hold values from -0.375 to 0.375
Outputs:
- layer_out: bfloat16 [2048, 8192], P(('branch', 'head'), 'page')
Inputs may be any that keep to these rules, and one draw needn't show every extreme that they name: `block_table`: each row names 4 distinct page ids; its first 1 entries are the same for every branch. `ancestor_len`: every branch's ancestors fill its first 1 pages; some branch reaches the maximum.
All inputs are finite; a program needn't handle non-finite values.
Results may differ from a plain program's by a relative error of at most 0.018.
Values may be sent and summed in bfloat16 or wider, within the bound.
A program may use at most 64 MiB of HBM per device.

v0:
```python
import math

import jax
import jax.numpy as jnp
from jax import lax
from jax.sharding import PartitionSpec as P

HD = 128
PAGE_TOK = 64
NEW = 256


masked_fill = -1e30


def attend(carried, queries_here, key_block, value_block, usable, score_scale):
    running_max, running_sum, accumulated = carried
    scores = (
        jnp.einsum("kbnd,jkd->kbnj", queries_here, key_block, preferred_element_type=jnp.float32)
        * score_scale
    )
    key_mask = usable[None, :, None, :]
    block_max = jnp.max(jnp.where(key_mask, scores, masked_fill), axis=-1)
    new_max = jnp.maximum(running_max, block_max)
    shrink = jnp.exp(running_max - new_max)
    weights = jnp.where(key_mask, jnp.exp(scores - new_max[..., None]), 0.0).astype(jnp.bfloat16)
    running_sum = running_sum * shrink + jnp.sum(weights.astype(jnp.float32), axis=-1)
    accumulated = accumulated * shrink[..., None] + jnp.einsum(
        "kbnj,jkd->kbnd", weights, value_block, preferred_element_type=jnp.float32
    )
    return (new_max, running_sum, accumulated)


def shards(
    queries, new_keys, new_values, cache_keys, cache_values, block_table, ancestor_len, out_weight
):
    row_count = queries.shape[0]
    branches_here = block_table.shape[0]
    slot_count = block_table.shape[1]
    heads_here = queries.shape[1] // HD
    kv_here = new_keys.shape[1] // HD
    group_size = heads_here // kv_here
    query_span = NEW * group_size
    score_scale = 1.0 / math.sqrt(HD)
    queries_here = (
        queries.reshape(branches_here, NEW, kv_here, group_size, HD)
        .transpose(2, 0, 1, 3, 4)
        .reshape(kv_here, branches_here, query_span, HD)
    )
    own_keys = new_keys.reshape(row_count, kv_here, HD)
    own_values = new_values.reshape(row_count, kv_here, HD)
    token_index = (
        jnp.arange(branches_here, dtype=jnp.int32)[:, None] * NEW
        + jnp.arange(query_span, dtype=jnp.int32)[None, :] // group_size
    )
    key_index = jnp.arange(row_count, dtype=jnp.int32)
    own_mask = (key_index[None, None, :] // NEW == token_index[:, :, None] // NEW) & (
        key_index[None, None, :] <= token_index[:, :, None]
    )
    own_scores = (
        jnp.einsum("kbnd,jkd->kbnj", queries_here, own_keys, preferred_element_type=jnp.float32)
        * score_scale
    )
    start_max = jnp.max(jnp.where(own_mask[None], own_scores, masked_fill), axis=-1)
    own_weights = jnp.where(own_mask[None], jnp.exp(own_scores - start_max[..., None]), 0.0).astype(
        jnp.bfloat16
    )
    start_sum = jnp.sum(own_weights.astype(jnp.float32), axis=-1)
    start_acc = jnp.einsum(
        "kbnj,jkd->kbnd", own_weights, own_values, preferred_element_type=jnp.float32
    )
    slot_first = jnp.arange(slot_count, dtype=jnp.int32) * PAGE_TOK
    slot_limit = jnp.clip(ancestor_len[:, None] - slot_first[None, :], 0, PAGE_TOK)
    carried = (start_max, start_sum, start_acc)
    piece_keys = lax.all_gather(cache_keys, ("branch", "page"), axis=0, tiled=True)
    piece_values = lax.all_gather(cache_values, ("branch", "page"), axis=0, tiled=True)
    page_count = piece_keys.shape[0]
    page_ids = jnp.arange(page_count, dtype=jnp.int32)
    slot_hits = block_table[:, :, None] == page_ids[None, None, :]
    live_tokens = jnp.sum(jnp.where(slot_hits, slot_limit[:, :, None], 0), axis=1)
    usable = jnp.arange(PAGE_TOK, dtype=jnp.int32)[None, None, :] < live_tokens[:, :, None]
    key_total = page_count * PAGE_TOK
    block_len = math.gcd(key_total, 512)
    block_count = key_total // block_len
    key_blocks = piece_keys.reshape(block_count, block_len, kv_here, HD)
    value_blocks = piece_values.reshape(block_count, block_len, kv_here, HD)
    usable_blocks = usable.reshape(branches_here, block_count, block_len).transpose(1, 0, 2)

    def block_step(state, block_item):
        key_block, value_block, usable_block = block_item
        state = attend(state, queries_here, key_block, value_block, usable_block, score_scale)
        return (state, None)

    carried, _ = lax.scan(block_step, carried, (key_blocks, value_blocks, usable_blocks))
    final_max, final_sum, final_acc = carried
    attn_out = (final_acc / final_sum[..., None]).reshape(
        kv_here, branches_here, NEW, group_size, HD
    )
    attn_out = (
        attn_out.transpose(1, 2, 0, 3, 4).reshape(row_count, heads_here * HD).astype(jnp.bfloat16)
    )
    partial_term = jnp.dot(
        lax.all_gather(attn_out, "page", axis=0, tiled=True),
        out_weight,
        preferred_element_type=jnp.float32,
    ).astype(jnp.bfloat16)
    summed = lax.psum_scatter(
        partial_term.astype(jnp.float32).astype(jnp.bfloat16),
        "head",
        scatter_dimension=0,
        tiled=True,
    )
    return summed


def solution(mesh):
    in_specs = (
        P(("branch", "page"), "head"),
        P(("branch", "page"), "head"),
        P(("branch", "page"), "head"),
        P(("branch", "page"), None, "head"),
        P(("branch", "page"), None, "head"),
        P(("branch", "page"), None),
        P(("branch", "page")),
        P("head", "page"),
    )
    out_specs = P(("branch", "head"), "page")
    return jax.shard_map(shards, mesh=mesh, in_specs=in_specs, out_specs=out_specs, check_vma=False)
```

profile of v0, /device:TPU:4, one launch (start us, length us, event | category | flops | bytes accessed | tf_op | source)
XLA Modules:
  0.0 155.8 jit_solution(14904132667431242414)
XLA Ops:
  6.5 0.0 copy-start
  6.5 0.0 all-gather.2.cloned.1.call-start
  6.6 1.3 reshape.378
  7.9 0.0 copy-start.1
  7.9 1.3 reshape_transpose_reshape.4
  9.2 9.3 %all_gather.9 = bf16[16,64,128]{2,1,0:T(8,128)(2,1)S(1)} all-gather(bf16[2,64,128]{2,1,0:T(8,128)(2,1)} %param.13), channel_id=1, replica_groups=mesh['branch'=2,'head'=4,'page'=4] {'branch','page'}, dimensions={0}, use_global_device_ids=true | all-gather | bytes 294912 | tf_op jit(solution)/shard_map/all_gather | solution.py:75
  18.5 8.5 %all_gather.10 = bf16[16,64,128]{2,1,0:T(8,128)(2,1)S(1)} all-gather(bf16[2,64,128]{2,1,0:T(8,128)(2,1)} %param.14), channel_id=1, replica_groups=mesh['branch'=2,'head'=4,'page'=4] {'branch','page'}, dimensions={0}, use_global_device_ids=true | all-gather | bytes 294912 | tf_op jit(solution)/shard_map/all_gather | solution.py:76
  27.7 0.7 select_reduce_fusion.2
  28.4 0.1 lt.34
  28.5 0.1 lt.35
  28.6 0.1 lt.32
  28.6 0.0 copy-done
  28.6 0.7 select_reduce_fusion.1
  29.3 0.7 convert_reduce_fusion.1
  30.0 0.0 copy-done.1
  30.0 0.5 convolution_bitcast_fusion.1
  30.5 7.0 %while.14 = (s32[]{:T(128)}, f32[1,1,2048]{2,1,0:T(1,128)S(1)}, f32[1,1,2048]{2,1,0:T(1,128)S(1)}, f32[1,1,2048,128]{3,2,1,0:T(8,128)S(1)}, pred[2,1,512]{2,1,0:...) while((s32[]{:T(128)}, f32[1,1,2048]{2,1,0:T(1,128)S(1)}, ...), condition=%wide.region_6.7_spmd, body=%wide.region_3.6_spmd.sunk | while | flops 551030784 | bytes 15600233 | solution.py:94
  30.6 0.8 select_reduce_fusion.4
  31.4 0.9 convert_reduce_fusion.3
  32.3 1.8 %fusion.24 = f32[1,1,2048,128]{3,2,1,0:T(8,128)S(1)} fusion(f32[1,1,2048,128]{3,2,1,0:T(8,128)S(1)} %get-tuple-element.169, f32[2048]{0:T(1024)S(1)} %bitcast.70, bf16[2,512,1,128]{3,1,2,0:T(8,128)(2,1)S(1)} %get-tuple-element.182, s32[]{:T(128)} %get-tuple-element.166, f32[512,2048]{1,0:T(8,128)S(1)} %get-tuple-element.154, f32[2048]{0:T(1024)S(1)} %bitcast.62, ...), kind=kOutput, calls=%fused_computation.4.clone.1 | convolution fusion | flops 273154048 | bytes 6439428 | tf_op jit(solution)/shard_map/while/body/eval_jaxpr/kbnj,jkd->kbnd/dot_general | solution.py:28
  34.1 0.8 select_reduce_fusion.4
  34.9 0.9 convert_reduce_fusion.3
  35.8 1.8 %fusion.24 = f32[1,1,2048,128]{3,2,1,0:T(8,128)S(1)} fusion(f32[1,1,2048,128]{3,2,1,0:T(8,128)S(1)} %get-tuple-element.169, f32[2048]{0:T(1024)S(1)} %bitcast.70, bf16[2,512,1,128]{3,1,2,0:T(8,128)(2,1)S(1)} %get-tuple-element.182, s32[]{:T(128)} %get-tuple-element.166, f32[512,2048]{1,0:T(8,128)S(1)} %get-tuple-element.154, f32[2048]{0:T(1024)S(1)} %bitcast.62, ...), kind=kOutput, calls=%fused_computation.4.clone.1 | convolution fusion | flops 273154048 | bytes 6439428 | tf_op jit(solution)/shard_map/while/body/eval_jaxpr/kbnj,jkd->kbnd/dot_general | solution.py:28
  37.6 0.3 divide_convert_fusion
  37.9 1.0 convert_element_type.28
  38.9 0.0 all-gather.2.cloned.1.call-update
  39.0 0.0 reduce-scatter.2.cloned.1.call-start
  39.0 22.6 %all-gather.2.cloned.1.call-done = bf16[1024,1024]{1,0:T(8,128)(2,1)} async-done(((bf16[256,1024]{1,0:T(8,128)(2,1)}), bf16[1024,1024]{1,0:T(8,128)(2,1)}) %all-gather.2.cloned.1.call-update) | async-done | bytes 2097168 | tf_op jit(solution)/shard_map/all_gather | solution.py:103
  61.6 9.2 %convolution_convert_fusion = bf16[1024,2048]{1,0:T(8,128)(2,1)} fusion(bf16[1024,1024]{1,0:T(8,128)(2,1)} %all-gather.2.cloned.1.call-done, bf16[1024,2048]{1,0:T(8,128)(2,1)} %param.17), kind=kOutput, calls=%fused_computation.16 | convolution fusion | flops 4297064448 | bytes 10485760 | tf_op jit(solution)/shard_map/dot_general | solution.py:102
  70.8 0.0 reduce-scatter.2.cloned.1.call-update
  70.9 78.1 %reduce-scatter.2.cloned.1.call-done = bf16[256,2048]{1,0:T(8,128)(2,1)} async-done(((bf16[1024,2048]{1,0:T(8,128)(2,1)}), bf16[256,2048]{1,0:T(8,128)(2,1)}) %reduce-scatter.2.cloned.1.call-update) | async-done | bytes 1048592 | tf_op jit(solution)/shard_map/reduce_scatter | solution.py:107
  (13 shorter events, 0.2 us)
Async XLA Ops:
  6.5 22.1 %copy-start = (bf16[256,128]{1,0:T(8,128)(2,1)S(1)}, bf16[256,128]{1,0:T(8,128)(2,1)}, u32[]{:S(2)}) copy-start(bf16[256,128]{1,0:T(8,128)(2,1)} %param.11) | copy-start | bytes 196612
  6.5 55.0 %all-gather.2.cloned.1.call-start = ((), (), s32[]{:S(2)}) async-start(), calls=%async_computation.1 | async-start | bytes 2621440 | tf_op jit(solution)/shard_map/all_gather | solution.py:103
  7.9 22.2 %copy-start.1 = (bf16[256,128]{1,0:T(8,128)(2,1)S(1)}, bf16[256,128]{1,0:T(8,128)(2,1)}, u32[]{:S(2)}) copy-start(bf16[256,128]{1,0:T(8,128)(2,1)} %param.12) | copy-start | bytes 196612
  39.0 109.9 %reduce-scatter.2.cloned.1.call-start = ((), (), s32[]{:S(2)}) async-start(), calls=%async_computation.2 | async-start | bytes 5242880 | tf_op jit(solution)/shard_map/reduce_scatter | solution.py:107
Sparse Core Ops, SparseCore 0:
  39.1 22.4 all-gather.1
  71.0 77.9 reduce-scatter.1
where the time goes:
time: 158 us; the launch traced here: 156 us
  waiting for transfers between devices  101 us (64%)
  blocking collectives  17.8 us (11%)
  matrix products  15.5 us (10%)
  between operations  14.1 us (9%)
  local copies, waits for them, and re-layouts  3.92 us (2%)
  other arithmetic  3.62 us (2%)
    reduce_scatter x1, waiting for transfers between devices, shards(): lax.psum_scatter(partial_term.astype(jnp.float32).astype(jnp.bfloat16), '...  78.1 us
    all_gather x1, waiting for transfers between devices, shards(): lax.all_gather(attn_out, 'page', axis=0, tiled=True)  22.6 us
    all_gather x1, blocking collectives, shards(): lax.all_gather(cache_keys, ('branch', 'page'), axis=0, tiled=True)  9.29 us
    dot_general x1, matrix products, shards(): jnp.dot(lax.all_gather(attn_out, 'page', axis=0, tiled=True), out_weight,...  9.24 us
    all_gather x1, blocking collectives, shards(): lax.all_gather(cache_values, ('branch', 'page'), axis=0, tiled=True)  8.53 us
    dot_general x2, matrix products, attend(): jnp.einsum('kbnj,jkd->kbnd', weights, value_block, preferred_element_type...  3.55 us
  transfers between devices with their start and end apart: 2, of which 2 were waited for; matrix products, arithmetic and copies ran while one was open for 0% of the time, Pallas kernels for 0%

commit v1 on v0

v1 whole, which is shorter than its diff:
```python
import functools
import math

import jax
import jax.numpy as jnp
from jax import lax
from jax.experimental import pallas as pl
from jax.experimental.pallas import tpu as pltpu
from jax.sharding import PartitionSpec as P

HD = 128
PAGE_TOK = 64
NEW = 256
PAIR = 2
MESH = pl.DeviceIdType.MESH


def kernel(
    n_branch,
    n_head,
    n_page,
    width,
    table_ref,
    len_ref,
    q_ref,
    nk_ref,
    nv_ref,
    ck_ref,
    cv_ref,
    w_hbm,
    out_ref,
    k_all,
    v_all,
    k_cat,
    v_cat,
    attn_all,
    w_ref,
    flow,
    total,
    w_sem,
    kv_send,
    kv_recv,
    attn_send,
    attn_recv,
    flow_send,
    flow_recv,
):
    my_branch = lax.axis_index("branch")
    z = lax.axis_index("head")
    my_page = lax.axis_index("page")
    group = n_branch * n_page
    me = my_branch * n_page + my_page
    rows = q_ref.shape[0]
    heads = q_ref.shape[1] // HD
    branches, slots = table_ref.shape
    pages_here = ck_ref.shape[0]
    ancestors = slots * PAGE_TOK
    span = ancestors + NEW
    rows_out, columns = out_ref.shape
    chunks = columns // width
    pairs = heads // PAIR

    w_copy = pltpu.make_async_copy(w_hbm, w_ref, w_sem)
    w_copy.start()

    def peer_of(k):
        other = lax.rem(me + k, group)
        return other // n_page, lax.rem(other, n_page)

    barrier = pltpu.get_barrier_semaphore()

    @pl.loop(1, group)
    def _(k):
        b, p = peer_of(k)
        pl.semaphore_signal(
            barrier, inc=1, device_id={"branch": b, "page": p}, device_id_type=MESH
        )

    @pl.when(z > 0)
    def _():
        pl.semaphore_signal(barrier, inc=1, device_id={"head": z - 1}, device_id_type=MESH)

    @pl.when(z < n_head - 1)
    def _():
        pl.semaphore_signal(barrier, inc=1, device_id={"head": z + 1}, device_id_type=MESH)

    inner_head = jnp.logical_and(z > 0, z < n_head - 1)
    pl.semaphore_wait(barrier, group - 1 + jnp.where(inner_head, 2, 1))

    def cache_copy(which, k):
        b, p = peer_of(k)
        src, dst = ((ck_ref, k_all), (cv_ref, v_all))[which]
        return pltpu.make_async_remote_copy(
            src_ref=src,
            dst_ref=dst.at[pl.ds(me * pages_here, pages_here)],
            send_sem=kv_send.at[which, k],
            recv_sem=kv_recv.at[which, k],
            device_id={"branch": b, "page": p},
            device_id_type=MESH,
        )

    @pl.loop(1, group)
    def _(k):
        cache_copy(0, k).start()
        cache_copy(1, k).start()

    k_all[pl.ds(me * pages_here, pages_here)] = ck_ref[...]
    v_all[pl.ds(me * pages_here, pages_here)] = cv_ref[...]
    v_cat[:, HD:] = jnp.ones((span, HD), jnp.bfloat16)

    def attn_copy(j, k):
        p = lax.rem(my_page + k, n_page)
        piece = attn_all.at[
            pl.ds(pl.multiple_of(my_page * rows, rows), rows),
            pl.ds(pl.multiple_of(j * PAIR * HD, PAIR * HD), PAIR * HD),
        ]
        return pltpu.make_async_remote_copy(
            src_ref=piece,
            dst_ref=piece,
            send_sem=attn_send.at[k, j],
            recv_sem=attn_recv.at[k, j],
            device_id={"page": p},
            device_id_type=MESH,
        )

    @pl.loop(1, group)
    def _(k):
        cache_copy(0, k).wait_recv()
        cache_copy(1, k).wait_recv()

    scale = math.log2(math.e) / math.sqrt(HD)
    column = lax.broadcasted_iota(jnp.int32, (NEW, span), 1)
    row = lax.broadcasted_iota(jnp.int32, (NEW, span), 0)

    for b in range(branches):
        for s in range(slots):
            page_id = table_ref[b, s]
            k_cat[s * PAGE_TOK : (s + 1) * PAGE_TOK] = k_all[page_id]
            v_cat[s * PAGE_TOK : (s + 1) * PAGE_TOK, :HD] = v_all[page_id]
        k_cat[ancestors:] = nk_ref[b * NEW : (b + 1) * NEW]
        v_cat[ancestors:, :HD] = nv_ref[b * NEW : (b + 1) * NEW]
        bound = jnp.where(column < ancestors, len_ref[b], ancestors + 1 + row)
        bias = jnp.where(column < bound, 0.0, -1e30).astype(jnp.float32)

        @pl.loop(0, pairs)
        def _(j):
            for h in range(PAIR):
                lanes = pl.ds(pl.multiple_of((j * PAIR + h) * HD, HD), HD)
                scores = lax.dot_general(
                    q_ref[b * NEW : (b + 1) * NEW, lanes],
                    k_cat[...],
                    (((1,), (1,)), ((), ())),
                    preferred_element_type=jnp.float32,
                )
                scores = scores * scale + bias
                top = jnp.max(scores, axis=-1, keepdims=True)
                numer = jnp.exp2(scores - top).astype(jnp.bfloat16)
                mixed = jnp.dot(numer, v_cat[...], preferred_element_type=jnp.float32)
                place = pl.ds(pl.multiple_of(my_page * rows + b * NEW, NEW), NEW)
                attn_all[place, lanes] = (mixed[:, :HD] / mixed[:, HD:]).astype(jnp.bfloat16)
            if b == branches - 1:

                @pl.loop(1, n_page)
                def _(k):
                    attn_copy(j, k).start()

    w_copy.wait()

    def flow_copy(d, c):
        down = jnp.where(d < z, 1, 0)
        return pltpu.make_async_remote_copy(
            src_ref=flow.at[down, d, c],
            dst_ref=flow.at[down, d, c],
            send_sem=flow_send.at[d, c],
            recv_sem=flow_recv.at[down, d, c],
            device_id={"head": jnp.where(d < z, z - 1, z + 1)},
            device_id_type=MESH,
        )

    def incoming(down, d, c):
        return pltpu.make_async_remote_copy(
            src_ref=flow.at[down, d, c],
            dst_ref=flow.at[down, d, c],
            send_sem=flow_send.at[d, c],
            recv_sem=flow_recv.at[down, d, c],
            device_id={"head": jnp.where(z == 0, z + 1, z - 1)},
            device_id_type=MESH,
        )

    phases = n_head // 2
    pages_phase = n_page // phases
    my_phase = my_page // pages_phase

    for ph in range(phases):
        half = lax.rem(my_phase + ph, phases)

        @pl.loop(0, pages_phase)
        def _(i):
            source = half * pages_phase + i
            k = lax.rem(my_page - source + n_page, n_page)

            @pl.when(k > 0)
            def _():
                @pl.loop(0, pairs)
                def _(j):
                    piece = attn_all.at[
                        pl.ds(pl.multiple_of(source * rows, rows), rows),
                        pl.ds(pl.multiple_of(j * PAIR * HD, PAIR * HD), PAIR * HD),
                    ]
                    pltpu.make_async_remote_copy(
                        src_ref=piece,
                        dst_ref=piece,
                        send_sem=attn_send.at[k, j],
                        recv_sem=attn_recv.at[k, j],
                        device_id={"page": lax.rem(my_page + 1, n_page)},
                        device_id_type=MESH,
                    ).wait_recv()

        @pl.loop(0, chunks * 2)
        def _(step):
            c = step // 2
            i = lax.rem(step, 2)
            d = half * 2 + jnp.where(z < n_head // 2, 1 - i, i)
            part = jnp.dot(
                attn_all[pl.ds(pl.multiple_of(d * rows_out, rows_out), rows_out), :],
                w_ref[:, pl.ds(pl.multiple_of(c * width, width), width)],
                preferred_element_type=jnp.float32,
            )
            down = jnp.where(d < z, 1, 0)
            received = jnp.where(d < z, z < n_head - 1, z > 0)

            @pl.when(d == z)
            def _():
                total[c] = part

            @pl.when(jnp.logical_and(d != z, received))
            def _():
                incoming(down, d, c).wait_recv()
                flow[down, d, c] = (part + flow[down, d, c].astype(jnp.float32)).astype(
                    jnp.bfloat16
                )
                flow_copy(d, c).start()

            @pl.when(jnp.logical_and(d != z, jnp.logical_not(received)))
            def _():
                flow[down, d, c] = part.astype(jnp.bfloat16)
                flow_copy(d, c).start()

    @pl.loop(0, chunks)
    def _(c):
        @pl.when(z > 0)
        def _():
            incoming(0, z, c).wait_recv()
            total[c] = total[c] + flow[0, z, c].astype(jnp.float32)

        @pl.when(z < n_head - 1)
        def _():
            incoming(1, z, c).wait_recv()
            total[c] = total[c] + flow[1, z, c].astype(jnp.float32)

        out_ref[:, pl.ds(pl.multiple_of(c * width, width), width)] = total[c].astype(
            jnp.bfloat16
        )

    @pl.loop(1, group)
    def _(k):
        cache_copy(0, k).wait_send()
        cache_copy(1, k).wait_send()

    @pl.loop(1, n_page)
    def _(k):
        @pl.loop(0, pairs)
        def _(j):
            attn_copy(j, k).wait_send()

    @pl.loop(0, n_head * chunks)
    def _(step):
        d = step // chunks
        c = lax.rem(step, chunks)

        @pl.when(d != z)
        def _():
            flow_copy(d, c).wait_send()


def solution(mesh):
    n_branch, n_head, n_page = (mesh.shape[a] for a in ("branch", "head", "page"))

    def shards(
        queries,
        new_keys,
        new_values,
        cache_keys,
        cache_values,
        block_table,
        ancestor_len,
        out_weight,
    ):
        rows, inner = queries.shape
        columns = out_weight.shape[1]
        rows_out = rows * n_page // n_head
        pages = cache_keys.shape[0] * n_branch * n_page
        span = block_table.shape[1] * PAGE_TOK + NEW
        width = math.gcd(columns, 256)
        chunks = columns // width
        pairs = inner // HD // PAIR
        group = n_branch * n_page
        vmem = pl.BlockSpec(memory_space=pltpu.VMEM)
        smem = pl.BlockSpec(memory_space=pltpu.SMEM)
        hbm = pl.BlockSpec(memory_space=pl.ANY)
        return pl.pallas_call(
            functools.partial(kernel, n_branch, n_head, n_page, width),
            out_shape=jax.ShapeDtypeStruct((rows_out, columns), jnp.bfloat16),
            in_specs=[smem, smem, vmem, vmem, vmem, vmem, vmem, hbm],
            out_specs=vmem,
            scratch_shapes=[
                pltpu.VMEM((pages, PAGE_TOK, HD), jnp.bfloat16),
                pltpu.VMEM((pages, PAGE_TOK, HD), jnp.bfloat16),
                pltpu.VMEM((span, HD), jnp.bfloat16),
                pltpu.VMEM((span, 2 * HD), jnp.bfloat16),
                pltpu.VMEM((rows * n_page, inner), jnp.bfloat16),
                pltpu.VMEM(out_weight.shape, jnp.bfloat16),
                pltpu.VMEM((2, n_head, chunks, rows_out, width), jnp.bfloat16),
                pltpu.VMEM((chunks, rows_out, width), jnp.float32),
                pltpu.SemaphoreType.DMA,
                pltpu.SemaphoreType.DMA((2, group)),
                pltpu.SemaphoreType.DMA((2, group)),
                pltpu.SemaphoreType.DMA((n_page, pairs)),
                pltpu.SemaphoreType.DMA((n_page, pairs)),
                pltpu.SemaphoreType.DMA((n_head, chunks)),
                pltpu.SemaphoreType.DMA((2, n_head, chunks)),
            ],
            compiler_params=pltpu.CompilerParams(
                collective_id=0, has_side_effects=True, vmem_limit_bytes=60 * 1024 * 1024
            ),
            cost_estimate=pl.CostEstimate(
                flops=2 * rows * n_page * inner * columns,
                bytes_accessed=2 * (inner * columns + rows_out * columns),
                transcendentals=0,
            ),
        )(
            block_table,
            ancestor_len,
            queries,
            new_keys,
            new_values,
            cache_keys,
            cache_values,
            out_weight,
        )

    in_specs = (
        P(("branch", "page"), "head"),
        P(("branch", "page"), "head"),
        P(("branch", "page"), "head"),
        P(("branch", "page"), None, "head"),
        P(("branch", "page"), None, "head"),
        P(("branch", "page"), None),
        P(("branch", "page")),
        P("head", "page"),
    )
    out_specs = P(("branch", "head"), "page")
    return jax.shard_map(shards, mesh=mesh, in_specs=in_specs, out_specs=out_specs, check_vma=False)
```

time: 158 us -> 118 us (0.75); the launches traced: 156 us -> 118 us
  Pallas kernels: 0 us -> 115 us
  waiting for transfers between devices: 101 us -> 0 us
  blocking collectives: 17.8 us -> 0 us
  matrix products: 15.5 us -> 0 us
  between operations: 14.1 us -> 0.66 us
  other arithmetic: 3.62 us -> 0 us
  local copies, waits for them, and re-layouts: 3.92 us -> 2.3 us
    pallas_call x0 -> x1, Pallas kernels: none -> 115 us  [shards(): pl.pallas_call(functools.partial(kernel, n_branch, n_head, n_page, width)...]
    reduce_scatter x1 -> x0, waiting for transfers between devices: 78.1 us -> none  [shards(): lax.psum_scatter(partial_term.astype(jnp.float32).astype(jnp.bfloat16), '...]
    all_gather x1 -> x0, waiting for transfers between devices: 22.6 us -> none  [shards(): lax.all_gather(attn_out, 'page', axis=0, tiled=True)]
    all_gather x2 -> x0, blocking collectives: 17.8 us -> none  [the longest x1 9.29 us: shards(): lax.all_gather(cache_keys, ('branch', 'page'), axis=0, tiled=True)]
    dot_general x7 -> x0, matrix products: 15.5 us -> none  [the longest x1 9.24 us: shards(): jnp.dot(lax.all_gather(attn_out, 'page', axis=0, tiled=True), out_weight,...]
    reduce_sum x4 -> x0, other arithmetic: 3.16 us -> none  [the longest x2 1.72 us: attend(): jnp.sum(weights.astype(jnp.float32), axis=-1)]
    another operation x2 -> x0, local copies, waits for them, and re-layouts: 2.6 us -> none  [the longest x1 1.3 us: shards(): queries_here = queries.reshape(branches_here, NEW, kv_here, group_size, H...]
    unnamed x4 -> x1, local copies, waits for them, and re-layouts: 0.01 us -> 2.3 us
  transfers between devices with their start and end apart: 2 -> 0, of which waited for: 2 -> 0; matrix products, arithmetic and copies ran while one was open for 0% -> 0% of each run, Pallas kernels for 0% -> 0%
where the time goes in v1:
time: 118 us
  Pallas kernels  115 us (97%)
  local copies, waits for them, and re-layouts  2.3 us (2%)
    pallas_call x1, Pallas kernels, shards(): pl.pallas_call(functools.partial(kernel, n_branch, n_head, n_page, width)...  115 us

profile of v1, /device:TPU:4, one launch (start us, length us, event | category | flops | bytes accessed | tf_op | source)
XLA Modules:
  0.0 118.1 jit_solution(542725494213285946)
XLA Ops:
  0.7 115.1 %shard_map.82 = bf16[256,2048]{1,0:T(8,128)(2,1)} custom-call(s32[1,4]{1,0:T(1,128)} %table_ref.1, s32[1]{0:T(128)S(6)} %copy.10.len_ref, bf16[256,1024]{1,0:T(8,128)(2,1)} %q_ref.1, bf16[256,128]{1,0:T(8,128)(2,1)} %nk_ref.1, bf16[256,128]{1,0:T(8,128)(2,1)} %nv_ref.1, bf16[2,64,128]{2,1,0:T(8,128)(2,1)} %ck_ref.1, bf16[2,64,128]{2,1,0:T(8,128)(2,1)} %cv_ref.1, ...), custom_call_target="tpu_custom_call" | custom-call | flops 4294967296 | bytes 5242880 | tf_op jit(solution)/shard_map/pallas_call | solution.py:311
  115.8 2.3 %copy.11 = bf16[256,2048]{1,0:T(8,128)(2,1)} copy(bf16[256,2048]{1,0:T(8,128)(2,1)} %shard_map.82) | data formatting | bytes 2097152

commit v2 on v1

--- a/solution.py
+++ b/solution.py
@@ -190,13 +190,28 @@
     phases = n_head // 2
     pages_phase = n_page // phases
     my_phase = my_page // pages_phase
-
-    for ph in range(phases):
-        half = lax.rem(my_phase + ph, phases)
-
-        @pl.loop(0, pages_phase)
+    ticks = (n_head - 1) * chunks
+
+    def stream(tick, going_down):
+        dest = piece = jnp.int32(0)
+        for first in range(phases):
+            start = 0
+            for ph in range(phases):
+                half = (first + ph) % phases
+                dests = [half * 2, half * 2 + 1] if going_down else [half * 2 + 1, half * 2]
+                dests = [d for d in dests if d != (n_head - 1 if going_down else 0)]
+                here = jnp.logical_and(my_phase == first, tick >= start)
+                local = jnp.maximum(tick - start, 0)
+                step = 1 if going_down else -1
+                dest = jnp.where(here, dests[0] + step * lax.rem(local, len(dests)), dest)
+                piece = jnp.where(here, local // len(dests), piece)
+                start += len(dests) * chunks
+        return dest, piece
+
+    def wait_attention(first, count):
+        @pl.loop(0, count)
         def _(i):
-            source = half * pages_phase + i
+            source = lax.rem(first + i, n_page)
             k = lax.rem(my_page - source + n_page, n_page)
 
             @pl.when(k > 0)
@@ -216,35 +231,54 @@
                         device_id_type=MESH,
                     ).wait_recv()
 
-        @pl.loop(0, chunks * 2)
-        def _(step):
-            c = step // 2
-            i = lax.rem(step, 2)
-            d = half * 2 + jnp.where(z < n_head // 2, 1 - i, i)
-            part = jnp.dot(
-                attn_all[pl.ds(pl.multiple_of(d * rows_out, rows_out), rows_out), :],
-                w_ref[:, pl.ds(pl.multiple_of(c * width, width), width)],
-                preferred_element_type=jnp.float32,
+    def project(d, c):
+        return jnp.dot(
+            attn_all[pl.ds(pl.multiple_of(d * rows_out, rows_out), rows_out), :],
+            w_ref[:, pl.ds(pl.multiple_of(c * width, width), width)],
+            preferred_element_type=jnp.float32,
+        )
+
+    def event(tick, down):
+        d, c = stream(tick, down)
+        active = d < z if down == 1 else d > z
+        received = z < n_head - 1 if down == 1 else z > 0
+        mine = jnp.logical_and(d == z, z == 0) if down == 1 else d == z
+
+        @pl.when(mine)
+        def _():
+            total[c] = project(d, c)
+
+        @pl.when(jnp.logical_and(active, received))
+        def _():
+            part = project(d, c)
+            incoming(down, d, c).wait_recv()
+            flow[down, d, c] = (part + flow[down, d, c].astype(jnp.float32)).astype(
+                jnp.bfloat16
             )
-            down = jnp.where(d < z, 1, 0)
-            received = jnp.where(d < z, z < n_head - 1, z > 0)
-
-            @pl.when(d == z)
+            flow_copy(d, c).start()
+
+        @pl.when(jnp.logical_and(active, jnp.logical_not(received)))
+        def _():
+            flow[down, d, c] = project(d, c).astype(jnp.bfloat16)
+            flow_copy(d, c).start()
+
+    def run(low, high):
+        @pl.loop(low, high)
+        def _(tick):
+            @pl.when(z < n_head // 2)
             def _():
-                total[c] = part
-
-            @pl.when(jnp.logical_and(d != z, received))
+                event(tick, 0)
+
+            event(tick, 1)
+
+            @pl.when(z >= n_head // 2)
             def _():
-                incoming(down, d, c).wait_recv()
-                flow[down, d, c] = (part + flow[down, d, c].astype(jnp.float32)).astype(
-                    jnp.bfloat16
-                )
-                flow_copy(d, c).start()
-
-            @pl.when(jnp.logical_and(d != z, jnp.logical_not(received)))
-            def _():
-                flow[down, d, c] = part.astype(jnp.bfloat16)
-                flow_copy(d, c).start()
+                event(tick, 0)
+
+    wait_attention(my_phase * pages_phase, pages_phase)
+    run(0, chunks)
+    wait_attention((my_phase + 1) * pages_phase, n_page - pages_phase)
+    run(chunks, ticks)
 
     @pl.loop(0, chunks)
     def _(c):

time: 118 us -> 104 us (0.88)
  Pallas kernels: 115 us -> 100 us
    pallas_call x1, Pallas kernels: 115 us -> 100 us  [shards(): pl.pallas_call(functools.partial(kernel, n_branch, n_head, n_page, width)...]
where the time goes in v2:
time: 104 us; the launch traced here: 103 us
  Pallas kernels  100 us (96%)
  local copies, waits for them, and re-layouts  2.3 us (2%)
    pallas_call x1, Pallas kernels, shards(): pl.pallas_call(functools.partial(kernel, n_branch, n_head, n_page, width)...  100 us
    unnamed x1, local copies, waits for them, and re-layouts  2.3 us

profile of v2, /device:TPU:4, one launch (start us, length us, event | category | flops | bytes accessed | tf_op | source)
XLA Modules:
  0.0 103.1 jit_solution(10094657757268858969)
XLA Ops:
  0.7 100.2 %shard_map.82 = bf16[256,2048]{1,0:T(8,128)(2,1)} custom-call(s32[1,4]{1,0:T(1,128)} %table_ref.1, s32[1]{0:T(128)S(6)} %copy.10.len_ref, bf16[256,1024]{1,0:T(8,128)(2,1)} %q_ref.1, bf16[256,128]{1,0:T(8,128)(2,1)} %nk_ref.1, bf16[256,128]{1,0:T(8,128)(2,1)} %nv_ref.1, bf16[2,64,128]{2,1,0:T(8,128)(2,1)} %ck_ref.1, bf16[2,64,128]{2,1,0:T(8,128)(2,1)} %cv_ref.1, ...), custom_call_target="tpu_custom_call" | custom-call | flops 4294967296 | bytes 5242880 | tf_op jit(solution)/shard_map/pallas_call | solution.py:345
  100.8 2.3 %copy.11 = bf16[256,2048]{1,0:T(8,128)(2,1)} copy(bf16[256,2048]{1,0:T(8,128)(2,1)} %shard_map.82) | data formatting | bytes 2097152

commit v3 on v2

--- a/solution.py
+++ b/solution.py
@@ -12,6 +12,7 @@
 PAGE_TOK = 64
 NEW = 256
 PAIR = 2
+SKEW = 2
 MESH = pl.DeviceIdType.MESH
 
 
@@ -33,6 +34,9 @@
     v_all,
     k_cat,
     v_cat,
+    v_own,
+    own_mix,
+    own_top,
     attn_all,
     w_ref,
     flow,
@@ -55,7 +59,6 @@
     branches, slots = table_ref.shape
     pages_here = ck_ref.shape[0]
     ancestors = slots * PAGE_TOK
-    span = ancestors + NEW
     rows_out, columns = out_ref.shape
     chunks = columns // width
     pairs = heads // PAIR
@@ -106,7 +109,42 @@
 
     k_all[pl.ds(me * pages_here, pages_here)] = ck_ref[...]
     v_all[pl.ds(me * pages_here, pages_here)] = cv_ref[...]
-    v_cat[:, HD:] = jnp.ones((span, HD), jnp.bfloat16)
+    v_cat[:, HD:] = jnp.ones((ancestors, HD), jnp.bfloat16)
+
+    scale = math.log2(math.e) / math.sqrt(HD)
+
+    def softmax_part(scores, floor):
+        top = jnp.max(scores, axis=-1, keepdims=True)
+        if floor is not None:
+            top = jnp.maximum(top, floor)
+        return top, jnp.exp2(scores - top).astype(jnp.bfloat16)
+
+    def scores_of(b, lanes, keys):
+        return scale * lax.dot_general(
+            q_ref[b * NEW : (b + 1) * NEW, lanes],
+            keys,
+            (((1,), (1,)), ((), ())),
+            preferred_element_type=jnp.float32,
+        )
+
+    own_row = lax.broadcasted_iota(jnp.int32, (NEW, NEW), 0)
+    own_column = lax.broadcasted_iota(jnp.int32, (NEW, NEW), 1)
+    own_bias = jnp.where(own_column <= own_row, 0.0, -1e30).astype(jnp.float32)
+
+    for b in range(branches):
+        v_own[b, :, :HD] = nv_ref[b * NEW : (b + 1) * NEW]
+        v_own[b, :, HD:] = jnp.ones((NEW, HD), jnp.bfloat16)
+
+        @pl.loop(0, pairs)
+        def _(j):
+            for h in range(PAIR):
+                head = j * PAIR + h
+                lanes = pl.ds(pl.multiple_of(head * HD, HD), HD)
+                top, numer = softmax_part(
+                    scores_of(b, lanes, nk_ref[b * NEW : (b + 1) * NEW]) + own_bias, None
+                )
+                own_mix[b, head] = jnp.dot(numer, v_own[b], preferred_element_type=jnp.float32)
+                own_top[b, head] = jnp.broadcast_to(top, (NEW, HD))
 
     def attn_copy(j, k):
         p = lax.rem(my_page + k, n_page)
@@ -128,34 +166,24 @@
         cache_copy(0, k).wait_recv()
         cache_copy(1, k).wait_recv()
 
-    scale = math.log2(math.e) / math.sqrt(HD)
-    column = lax.broadcasted_iota(jnp.int32, (NEW, span), 1)
-    row = lax.broadcasted_iota(jnp.int32, (NEW, span), 0)
+    column = lax.broadcasted_iota(jnp.int32, (NEW, ancestors), 1)
 
     for b in range(branches):
         for s in range(slots):
             page_id = table_ref[b, s]
             k_cat[s * PAGE_TOK : (s + 1) * PAGE_TOK] = k_all[page_id]
             v_cat[s * PAGE_TOK : (s + 1) * PAGE_TOK, :HD] = v_all[page_id]
-        k_cat[ancestors:] = nk_ref[b * NEW : (b + 1) * NEW]
-        v_cat[ancestors:, :HD] = nv_ref[b * NEW : (b + 1) * NEW]
-        bound = jnp.where(column < ancestors, len_ref[b], ancestors + 1 + row)
-        bias = jnp.where(column < bound, 0.0, -1e30).astype(jnp.float32)
+        bias = jnp.where(column < len_ref[b], 0.0, -1e30).astype(jnp.float32)
 
         @pl.loop(0, pairs)
         def _(j):
             for h in range(PAIR):
-                lanes = pl.ds(pl.multiple_of((j * PAIR + h) * HD, HD), HD)
-                scores = lax.dot_general(
-                    q_ref[b * NEW : (b + 1) * NEW, lanes],
-                    k_cat[...],
-                    (((1,), (1,)), ((), ())),
-                    preferred_element_type=jnp.float32,
-                )
-                scores = scores * scale + bias
-                top = jnp.max(scores, axis=-1, keepdims=True)
-                numer = jnp.exp2(scores - top).astype(jnp.bfloat16)
+                head = j * PAIR + h
+                lanes = pl.ds(pl.multiple_of(head * HD, HD), HD)
+                before = own_top[b, head][:, :1]
+                top, numer = softmax_part(scores_of(b, lanes, k_cat[...]) + bias, before)
                 mixed = jnp.dot(numer, v_cat[...], preferred_element_type=jnp.float32)
+                mixed = mixed + own_mix[b, head] * jnp.exp2(before - top)
                 place = pl.ds(pl.multiple_of(my_page * rows + b * NEW, NEW), NEW)
                 attn_all[place, lanes] = (mixed[:, :HD] / mixed[:, HD:]).astype(jnp.bfloat16)
             if b == branches - 1:
@@ -238,11 +266,16 @@
             preferred_element_type=jnp.float32,
         )
 
-    def event(tick, down):
+    def event(step, down):
+        depth = n_head - 1 - z if down == 1 else z
+        tick = step - SKEW * jnp.maximum(depth - 1, 0)
         d, c = stream(tick, down)
-        active = d < z if down == 1 else d > z
+        valid = jnp.logical_and(tick >= 0, tick < ticks)
+        active = jnp.logical_and(valid, d < z if down == 1 else d > z)
         received = z < n_head - 1 if down == 1 else z > 0
-        mine = jnp.logical_and(d == z, z == 0) if down == 1 else d == z
+        mine = jnp.logical_and(valid, d == z)
+        if down == 1:
+            mine = jnp.logical_and(mine, z == 0)
 
         @pl.when(mine)
         def _():
@@ -264,21 +297,21 @@
 
     def run(low, high):
         @pl.loop(low, high)
-        def _(tick):
+        def _(step):
             @pl.when(z < n_head // 2)
             def _():
-                event(tick, 0)
-
-            event(tick, 1)
+                event(step, 0)
+
+            event(step, 1)
 
             @pl.when(z >= n_head // 2)
             def _():
-                event(tick, 0)
+                event(step, 0)
 
     wait_attention(my_phase * pages_phase, pages_phase)
     run(0, chunks)
     wait_attention((my_phase + 1) * pages_phase, n_page - pages_phase)
-    run(chunks, ticks)
+    run(chunks, ticks + SKEW * (n_head - 2))
 
     @pl.loop(0, chunks)
     def _(c):
@@ -334,7 +367,9 @@
         columns = out_weight.shape[1]
         rows_out = rows * n_page // n_head
         pages = cache_keys.shape[0] * n_branch * n_page
-        span = block_table.shape[1] * PAGE_TOK + NEW
+        ancestors = block_table.shape[1] * PAGE_TOK
+        branches = block_table.shape[0]
+        heads = inner // HD
         width = math.gcd(columns, 256)
         chunks = columns // width
         pairs = inner // HD // PAIR
@@ -350,8 +385,11 @@
             scratch_shapes=[
                 pltpu.VMEM((pages, PAGE_TOK, HD), jnp.bfloat16),
                 pltpu.VMEM((pages, PAGE_TOK, HD), jnp.bfloat16),
-                pltpu.VMEM((span, HD), jnp.bfloat16),
-                pltpu.VMEM((span, 2 * HD), jnp.bfloat16),
+                pltpu.VMEM((ancestors, HD), jnp.bfloat16),
+                pltpu.VMEM((ancestors, 2 * HD), jnp.bfloat16),
+                pltpu.VMEM((branches, NEW, 2 * HD), jnp.bfloat16),
+                pltpu.VMEM((branches, heads, NEW, 2 * HD), jnp.float32),
+                pltpu.VMEM((branches, heads, NEW, HD), jnp.float32),
                 pltpu.VMEM((rows * n_page, inner), jnp.bfloat16),
                 pltpu.VMEM(out_weight.shape, jnp.bfloat16),
                 pltpu.VMEM((2, n_head, chunks, rows_out, width), jnp.bfloat16),

time: 104 us -> 100 us (0.962)
  Pallas kernels: 100 us -> 97 us
    pallas_call x1, Pallas kernels: 100 us -> 97 us  [shards(): pl.pallas_call(functools.partial(kernel, n_branch, n_head, n_page, width)...]
where the time goes in v3:
time: 100 us; the launch traced here: 99.9 us
  Pallas kernels  97 us (97%)
  local copies, waits for them, and re-layouts  2.3 us (2%)
    pallas_call x1, Pallas kernels, shards(): pl.pallas_call(functools.partial(kernel, n_branch, n_head, n_page, width)...  97 us
    unnamed x1, local copies, waits for them, and re-layouts  2.3 us

profile of v3, /device:TPU:4, one launch (start us, length us, event | category | flops | bytes accessed | tf_op | source)
XLA Modules:
  0.0 99.9 jit_solution(9783006644030688994)
XLA Ops:
  0.7 97.0 %shard_map.82 = bf16[256,2048]{1,0:T(8,128)(2,1)} custom-call(s32[1,4]{1,0:T(1,128)} %table_ref.1, s32[1]{0:T(128)S(6)} %copy.10.len_ref, bf16[256,1024]{1,0:T(8,128)(2,1)} %q_ref.1, bf16[256,128]{1,0:T(8,128)(2,1)} %nk_ref.1, bf16[256,128]{1,0:T(8,128)(2,1)} %nv_ref.1, bf16[2,64,128]{2,1,0:T(8,128)(2,1)} %ck_ref.1, bf16[2,64,128]{2,1,0:T(8,128)(2,1)} %cv_ref.1, ...), custom_call_target="tpu_custom_call" | custom-call | flops 4294967296 | bytes 5242880 | tf_op jit(solution)/shard_map/pallas_call | solution.py:380
  97.6 2.3 %copy.11 = bf16[256,2048]{1,0:T(8,128)(2,1)} copy(bf16[256,2048]{1,0:T(8,128)(2,1)} %shard_map.82) | data formatting | bytes 2097152

commit v4 on v3

--- a/solution.py
+++ b/solution.py
@@ -231,8 +231,8 @@
                 here = jnp.logical_and(my_phase == first, tick >= start)
                 local = jnp.maximum(tick - start, 0)
                 step = 1 if going_down else -1
-                dest = jnp.where(here, dests[0] + step * lax.rem(local, len(dests)), dest)
-                piece = jnp.where(here, local // len(dests), piece)
+                dest = jnp.where(here, dests[0] + step * jnp.minimum(local // chunks, len(dests) - 1), dest)
+                piece = jnp.where(here, lax.rem(local, chunks), piece)
                 start += len(dests) * chunks
         return dest, piece
 

time: 100 us -> 97 us (0.970)
  the two profiles are of different devices: /device:TPU:4 before, /device:TPU:12 now
where the time goes in v4:
time: 97 us; the launch traced here: 96.8 us
  Pallas kernels  93.8 us (97%)
  local copies, waits for them, and re-layouts  2.3 us (2%)
    pallas_call x1, Pallas kernels, shards(): pl.pallas_call(functools.partial(kernel, n_branch, n_head, n_page, width)...  93.8 us
    unnamed x1, local copies, waits for them, and re-layouts  2.3 us

profile of v4, /device:TPU:12, one launch (start us, length us, event | category | flops | bytes accessed | tf_op | source)
XLA Modules:
  0.0 96.8 jit_solution(15424854185426819576)
XLA Ops:
  0.7 93.8 %shard_map.82 = bf16[256,2048]{1,0:T(8,128)(2,1)} custom-call(s32[1,4]{1,0:T(1,128)} %table_ref.1, s32[1]{0:T(128)S(6)} %copy.10.len_ref, bf16[256,1024]{1,0:T(8,128)(2,1)} %q_ref.1, bf16[256,128]{1,0:T(8,128)(2,1)} %nk_ref.1, bf16[256,128]{1,0:T(8,128)(2,1)} %nv_ref.1, bf16[2,64,128]{2,1,0:T(8,128)(2,1)} %ck_ref.1, bf16[2,64,128]{2,1,0:T(8,128)(2,1)} %cv_ref.1, ...), custom_call_target="tpu_custom_call" | custom-call | flops 4294967296 | bytes 5242880 | tf_op jit(solution)/shard_map/pallas_call | solution.py:380
  94.5 2.3 %copy.11 = bf16[256,2048]{1,0:T(8,128)(2,1)} copy(bf16[256,2048]{1,0:T(8,128)(2,1)} %shard_map.82) | data formatting | bytes 2097152

commit v5 on v4

--- a/solution.py
+++ b/solution.py
@@ -30,6 +30,7 @@
     cv_ref,
     w_hbm,
     out_ref,
+    late_ref,
     k_all,
     v_all,
     k_cat,
@@ -315,6 +316,8 @@
 
     @pl.loop(0, chunks)
     def _(c):
+        lanes = pl.ds(pl.multiple_of(c * width, width), width)
+
         @pl.when(z > 0)
         def _():
             incoming(0, z, c).wait_recv()
@@ -323,11 +326,13 @@
         @pl.when(z < n_head - 1)
         def _():
             incoming(1, z, c).wait_recv()
-            total[c] = total[c] + flow[1, z, c].astype(jnp.float32)
-
-        out_ref[:, pl.ds(pl.multiple_of(c * width, width), width)] = total[c].astype(
-            jnp.bfloat16
-        )
+            late_ref[:, lanes] = flow[1, z, c]
+
+        @pl.when(z == n_head - 1)
+        def _():
+            late_ref[:, lanes] = jnp.zeros((rows_out, width), jnp.bfloat16)
+
+        out_ref[:, lanes] = total[c].astype(jnp.bfloat16)
 
     @pl.loop(1, group)
     def _(k):
@@ -377,11 +382,11 @@
         vmem = pl.BlockSpec(memory_space=pltpu.VMEM)
         smem = pl.BlockSpec(memory_space=pltpu.SMEM)
         hbm = pl.BlockSpec(memory_space=pl.ANY)
-        return pl.pallas_call(
+        early, late = pl.pallas_call(
             functools.partial(kernel, n_branch, n_head, n_page, width),
-            out_shape=jax.ShapeDtypeStruct((rows_out, columns), jnp.bfloat16),
+            out_shape=[jax.ShapeDtypeStruct((rows_out, columns), jnp.bfloat16)] * 2,
             in_specs=[smem, smem, vmem, vmem, vmem, vmem, vmem, hbm],
-            out_specs=vmem,
+            out_specs=[vmem, vmem],
             scratch_shapes=[
                 pltpu.VMEM((pages, PAGE_TOK, HD), jnp.bfloat16),
                 pltpu.VMEM((pages, PAGE_TOK, HD), jnp.bfloat16),
@@ -420,6 +425,7 @@
             cache_values,
             out_weight,
         )
+        return (early.astype(jnp.float32) + late.astype(jnp.float32)).astype(jnp.bfloat16)
 
     in_specs = (
         P(("branch", "page"), "head"),

time: 97 us -> 97.9 us (level)
  other arithmetic: 0 us -> 2.91 us
  local copies, waits for them, and re-layouts: 2.3 us -> 0 us
    convert_element_type x0 -> x1, other arithmetic: none -> 2.91 us  [shards(): (early.astype(jnp.float32) + late.astype(jnp.float32)).astype(jnp.bfloat16)]
    unnamed x1 -> x0, local copies, waits for them, and re-layouts: 2.3 us -> none
where the time goes in v5:
time: 97.9 us; the launch traced here: 97.8 us
  Pallas kernels  94.2 us (96%)
  other arithmetic  2.91 us (3%)
    pallas_call x1, Pallas kernels, shards(): pl.pallas_call(functools.partial(kernel, n_branch, n_head, n_page, width)...  94.2 us
    convert_element_type x1, other arithmetic, shards(): (early.astype(jnp.float32) + late.astype(jnp.float32)).astype(jnp.bfloat16)  2.91 us

profile of v5, /device:TPU:12, one launch (start us, length us, event | category | flops | bytes accessed | tf_op | source)
XLA Modules:
  0.0 97.8 jit_solution(3009091518638393268)
XLA Ops:
  0.7 94.2 %shard_map.82 = (bf16[256,2048]{1,0:T(8,128)(2,1)}, bf16[256,2048]{1,0:T(8,128)(2,1)}) custom-call(s32[1,4]{1,0:T(1,128)} %table_ref.1, s32[1]{0:T(128)S(6)} %copy.9.len_ref, bf16[256,1024]{1,0:T(8,128)(2,1)} %q_ref.1, bf16[256,128]{1,0:T(8,128)(2,1)} %nk_ref.1, bf16[256,128]{1,0:T(8,128)(2,1)} %nv_ref.1, bf16[2,64,128]{2,1,0:T(8,128)(2,1)} %ck_ref.1, ...), custom_call_target="tpu_custom_call" | custom-call | flops 4294967296 | bytes 5242880 | tf_op jit(solution)/shard_map/pallas_call | solution.py:385
  94.9 2.9 %add_convert_fusion = bf16[256,2048]{1,0:T(8,128)(2,1)} fusion(bf16[256,2048]{1,0:T(8,128)(2,1)} %get-tuple-element.8, bf16[256,2048]{1,0:T(8,128)(2,1)} %get-tuple-element.7), kind=kLoop, calls=%fused_computation | loop fusion | flops 2097152 | bytes 3145728 | tf_op jit(solution)/shard_map/convert_element_type | solution.py:428
